TPU v7x, 32 devices: a whole 2x2x4 slice. The times are simulated.
32 devices in a mesh: group: 4 (over y, core), dev: 8 (over z, x).
Axes of the slice: x: 2, y: 2, z: 4, core: 2. Of those that a mesh axis runs over, the one named last changes fastest.
Arguments:
- node_state: bfloat16 [16384, 512], P(('group', 'dev')), may hold values from -6 to 6
- hub_state: bfloat16 [64, 512], P('dev'), may hold values from -6 to 6
- w_edge_in: bfloat16 [512, 256], replicated, may hold values from -0.25 to 0.25
- w_edge_out: bfloat16 [256, 512], replicated, may hold values from -0.375 to 0.375
- w_update: bfloat16 [512, 512], replicated, may hold values from -0.25 to 0.25
- edge_src: int32 [131072], P(('group', 'dev')), may hold values from 0 to 319
- edge_dst: int32 [131072], P(('group', 'dev')), may hold values from 0 to 319
- edge_mask: int32 [131072], P(('group', 'dev')), may hold values 0 or 1
- send_list: int32 [32, 8, 32], P(('group', 'dev')), may hold values from 0 to 511
- send_count: int32 [32, 8], P(('group', 'dev')), may hold values from 8 to 32, as said below
- node_cot: bfloat16 [16384, 512], P(('group', 'dev')), may hold values from -0.059814453 to 0.059814453
- hub_cot: bfloat16 [64, 512], P('dev'), may hold values from -0.059814453 to 0.059814453
Outputs:
- new_state: bfloat16 [16384, 512], P(('group', 'dev'))
- new_hub: bfloat16 [64, 512], P('dev')
- grad_in: float32 [512, 256], replicated
- grad_out: float32 [256, 512], replicated
- grad_update: float32 [512, 512], replicated
Inputs may be any that keep to these rules, and one draw needn't show every extreme that they name: Device 0 sends 32 live slots to peer 0: send_count[0, 0] = 32.
All inputs are finite; a program needn't handle non-finite values. No bound on the sum of `edge_mask` on one device may be relied on, other than what follows from the above.
Results may differ from a plain program's by a relative error of at most 0.0064.
The roundings to bfloat16 on the way count: a program that leaves them out, or rounds other values in their place, can miss the bound.
Values may be sent and summed in bfloat16 or wider, within the bound.
No kernel may reach another device: no remote copies, remote signals or barrier semaphores. Data moves between devices by JAX's collectives and lax.ppermute only.
A program may use at most 64 MiB of HBM per device.

v0:
```python
import jax
import jax.numpy as jnp
from jax import lax
from jax.sharding import PartitionSpec as P

F32 = jnp.float32
BF16 = jnp.bfloat16


def silu_grad(values):
    sigmoid_v = jax.nn.sigmoid(values)
    return sigmoid_v * (1.0 + values * (1.0 - sigmoid_v))


def dot(left, right, dims=((1,), (0,))):
    return lax.dot_general(left, right, (dims, ((), ())), preferred_element_type=F32)


def split_dot(left, right, dims):
    high = left.astype(BF16)
    low = (left - high.astype(F32)).astype(BF16)
    return dot(high, right, dims) + dot(low, right, dims)


def swap(blocks, axis, size, stride, total):
    position = lax.rem(lax.div(lax.axis_index(axis), stride), size)
    if size == 2:
        pairs = [(i, i ^ stride) for i in range(total)]
        other = lax.ppermute(lax.dynamic_index_in_dim(blocks, 1 - position, 0, False), axis, pairs)
        own = lax.dynamic_index_in_dim(blocks, position, 0, False)
        first = position == 0
        return jnp.stack([jnp.where(first, own, other), jnp.where(first, other, own)])
    if size * stride == total and stride == 1:
        groups = None
    else:
        groups = [
            [base + off + i * stride for i in range(size)]
            for base in range(0, total, size * stride)
            for off in range(stride)
        ]
    return lax.all_to_all(blocks, axis, 0, 0, tiled=True, axis_index_groups=groups)


def scatter_sum(value, axis, size, stride, total):
    position = lax.rem(lax.div(lax.axis_index(axis), stride), size)
    blocks = value.reshape(size, -1, value.shape[1])
    if size == 2:
        pairs = [(i, i ^ stride) for i in range(total)]
        sent = lax.dynamic_index_in_dim(blocks, 1 - position, 0, False).astype(BF16)
        own = lax.dynamic_index_in_dim(blocks, position, 0, False)
        return own + lax.ppermute(sent, axis, pairs).astype(F32)
    return jnp.sum(swap(blocks.astype(BF16), axis, size, stride, total).astype(F32), axis=0)


def gather_all(value, axis, size, stride, total):
    spread = jnp.broadcast_to(value[None], (size,) + value.shape)
    return swap(spread, axis, size, stride, total).reshape(-1, value.shape[1])


def shards(
    node_state,
    hub_state,
    w_edge_in,
    w_edge_out,
    w_update,
    edge_src,
    edge_dst,
    edge_mask,
    send_list,
    send_count,
    node_cot,
    hub_cot,
    *,
    n_group,
    n_dev
):
    width = node_state.shape[1]
    hidden_width = w_edge_in.shape[1]
    master_rows = node_state.shape[0]
    send_rows = send_list[0]
    slot_width = send_rows.shape[1]
    mirror_total = n_dev * slot_width
    hub_rows = hub_state.shape[0]
    live_slot = jnp.arange(slot_width)[None, :] < send_count[0][:, None]
    chosen = jnp.where(live_slot, send_rows, -1).reshape(1, -1)
    select = (jnp.arange(master_rows)[:, None] == chosen).astype(BF16)
    outgoing = dot(select, node_state, ((0,), (0,))).astype(BF16)
    packed = jnp.concatenate(
        [
            outgoing.reshape(n_dev, slot_width, width),
            jnp.broadcast_to(hub_state[None], (n_dev, hub_rows, width)),
        ],
        axis=1,
    )
    arrived = lax.all_to_all(packed, "dev", 0, 0, tiled=True)
    table = jnp.concatenate(
        [
            arrived[:, :slot_width].reshape(mirror_total, width),
            arrived[:, slot_width:].reshape(-1, width),
        ],
        axis=0,
    )
    local_rows = table.shape[0]
    ids = jnp.arange(local_rows)[:, None]
    from_hot = (ids == edge_src[None, :]).astype(BF16)
    to_hot = (ids == jnp.where(edge_mask > 0, edge_dst, -1)[None, :]).astype(BF16)
    adjacency = dot(to_hot, from_hot, ((1,), (1,)))
    adj_high = jnp.floor(adjacency * (1.0 / 256.0))
    adj_low = (adjacency - 256.0 * adj_high).astype(BF16)
    adj_high = adj_high.astype(BF16)
    counts = jnp.sum(adjacency, axis=1)
    pre_act = dot(table, w_edge_in)
    hidden = jax.nn.silu(pre_act).astype(BF16)
    partial = dot(adj_low, hidden) + 256.0 * dot(adj_high, hidden)

    def by_peer(value, hubs_of):
        return jnp.concatenate(
            [
                value[:mirror_total].reshape((n_dev, slot_width) + value.shape[1:]),
                value[mirror_total:].reshape((n_dev, hubs_of) + value.shape[1:]),
            ],
            axis=1,
        )

    rounded_count = counts.astype(BF16)
    rest_count = (counts - rounded_count.astype(F32)).astype(BF16)
    count_rows = jnp.stack(
        [by_peer(rounded_count, hub_rows), by_peer(rest_count, hub_rows)], axis=1
    )
    count_rows = jnp.pad(count_rows, ((0, 0), (0, 6), (0, hidden_width - slot_width - hub_rows)))
    message = jnp.concatenate([by_peer(partial.astype(BF16), hub_rows), count_rows], axis=1)
    back = lax.all_to_all(message, "dev", 0, 0, tiled=True)
    base = slot_width + hub_rows
    back_part = back[:, :slot_width].reshape(mirror_total, hidden_width)
    back_count = back[:, base, :slot_width].reshape(mirror_total, 1)
    summed_hidden = dot(select, back_part)
    degree = dot(select, back_count)
    hub_hidden = jnp.sum(back[:, slot_width:base].astype(F32), axis=0)
    hub_degree = jnp.sum(back[:, base : base + 2, slot_width:base].astype(F32), axis=(0, 1))
    hub_sums = jnp.concatenate(
        [hub_hidden, jnp.broadcast_to(hub_degree[:, None], (hub_rows, 128))], axis=1
    )
    hub_sums = lax.psum(hub_sums, "group")
    hub_hidden, hub_degree = (
        hub_sums[:, :hidden_width],
        hub_sums[:, hidden_width : hidden_width + 1],
    )
    states = jnp.concatenate([node_state, hub_state], axis=0).astype(F32)
    cotangent = jnp.concatenate([node_cot, hub_cot], axis=0).astype(F32)
    degree = jnp.maximum(jnp.concatenate([degree, hub_degree], axis=0), 1.0)
    summed_hidden = jnp.concatenate([summed_hidden, hub_hidden], axis=0)
    summed = split_dot(summed_hidden, w_edge_out, ((1,), (0,)))
    mixed = (states + summed / degree).astype(BF16)
    pre_update = dot(mixed, w_update)
    updated = (states + jax.nn.silu(pre_update)).astype(BF16)
    grad_pre = (cotangent * silu_grad(pre_update)).astype(BF16)
    grad_sum = (dot(grad_pre, w_update, ((1,), (1,))) / degree).astype(BF16)
    grad_hidden = dot(grad_sum, w_edge_out, ((1,), (1,))).astype(BF16)
    grad_outgoing = dot(select, grad_hidden[:master_rows], ((0,), (0,))).astype(BF16)
    packed_grad = jnp.concatenate(
        [
            grad_outgoing.reshape(n_dev, slot_width, hidden_width),
            jnp.broadcast_to(grad_hidden[None, master_rows:], (n_dev, hub_rows, hidden_width)),
        ],
        axis=1,
    )
    arrived_grad = lax.all_to_all(packed_grad, "dev", 0, 0, tiled=True)
    grad_rows = jnp.concatenate(
        [
            arrived_grad[:, :slot_width].reshape(mirror_total, hidden_width),
            arrived_grad[:, slot_width:].reshape(-1, hidden_width),
        ],
        axis=0,
    )
    row_weight = jnp.where(
        jnp.arange(mixed.shape[0])[:, None] < master_rows,
        1.0,
        (lax.axis_index("group") == 0).astype(F32),
    )
    weighted = (grad_pre.astype(F32) * row_weight).astype(BF16)
    grad_update = dot(mixed, weighted, ((0,), (0,)))
    grad_out = split_dot(summed_hidden * row_weight, grad_sum, ((0,), (0,)))
    by_source = dot(adj_low, grad_rows, ((0,), (0,))) + 256.0 * dot(
        adj_high, grad_rows, ((0,), (0,))
    )
    grad_act = by_source * silu_grad(pre_act)
    act_high = grad_act.astype(BF16)
    act_low = (grad_act - act_high.astype(F32)).astype(BF16)
    grad_in = dot(table, act_high, ((0,), (0,))) + dot(table, act_low, ((0,), (0,)))
    half = width // 2
    side = jnp.concatenate([grad_in[:half], grad_in[half:]], axis=1)
    whole = jnp.concatenate([grad_update, grad_out, side], axis=0)
    whole = scatter_sum(whole, "group", 2, 1, n_group)
    whole = scatter_sum(whole, "group", n_group // 2, 2, n_group)
    whole = scatter_sum(whole, "dev", n_dev, 1, n_dev)
    whole = gather_all(whole.astype(BF16), "dev", n_dev, 1, n_dev)
    whole = gather_all(whole, "group", n_group // 2, 2, n_group)
    whole = gather_all(whole, "group", 2, 1, n_group).astype(F32)
    side = whole[width + hidden_width :]
    return (
        updated[:master_rows],
        updated[master_rows:],
        jnp.concatenate([side[:, :hidden_width], side[:, hidden_width:]], axis=0),
        whole[width : width + hidden_width],
        whole[:width],
    )


def solution(mesh):

    def body(*args):
        return shards(*args, n_group=mesh.shape["group"], n_dev=mesh.shape["dev"])

    return jax.shard_map(
        body,
        mesh=mesh,
        in_specs=(
            P(("group", "dev"), None),
            P("dev", None),
            P(),
            P(),
            P(),
            P(("group", "dev")),
            P(("group", "dev")),
            P(("group", "dev")),
            P(("group", "dev"), None, None),
            P(("group", "dev"), None),
            P(("group", "dev"), None),
            P("dev", None),
        ),
        out_specs=(P(("group", "dev"), None), P("dev", None), P(), P(), P()),
        check_vma=False,
    )
```

profile of v0, /device:TPU:0, one launch (start us, length us, event | category | flops | bytes accessed | tf_op | source)
XLA Modules:
  0.0 114.2 jit_solution(3356900994865378915)
XLA Ops:
  0.6 0.8 iota_compare_fusion.11
  1.5 0.8 squeeze.19
  2.3 1.4 %convolution_convert_fusion.1 = bf16[256,512]{1,0:T(8,128)(2,1)S(1)} fusion(bf16[512,512]{1,0:T(8,128)(2,1)} %param.12, s32[256]{0:T(256)S(1)} %broadcast_select_fusion), kind=kOutput, calls=%fused_computation.16 | convolution fusion | flops 134479872 | bytes 787456 | tf_op jit(solution)/shard_map/dot_general | solution.py:16
  3.7 0.7 broadcast_in_dim.28
  4.4 0.7 pad_maximum_fusion.4
  5.2 7.3 %all-to-all-start = ((bf16[8,40,512]{2,1,0:T(8,128)(2,1)}), bf16[8,40,512]{2,1,0:T(8,128)(2,1)S(1)}, u32[]{:S(2)}, u32[]{:S(2)}) async-start(bf16[8,40,512]{2,1,0:T(8,128)(2,1)} %pad_maximum_fusion.4), calls=%async_computation | async-start | bytes 655360 | tf_op jit(solution)/shard_map/all_to_all | solution.py:95
  12.5 2.0 %fusion.62 = (f32[320]{0:T(512)S(1)}, f32[320,320]{0,1:T(8,128)S(1)}) fusion(s32[4096]{0:T(1024)S(1)} %copy-done.13, s32[4096]{0:T(1024)S(1)} %compare_select_fusion), kind=kOutput, calls=%fused_computation.120 | convolution fusion | flops 841584320 | bytes 443648 | tf_op jit(solution)/shard_map/dot_general | solution.py:16
  14.8 8.0 %all-to-all-done = bf16[8,40,512]{2,1,0:T(8,128)(2,1)S(1)} async-done(((bf16[8,40,512]{2,1,0:T(8,128)(2,1)}), bf16[8,40,512]{2,1,0:T(8,128)(2,1)S(1)}, u32[]{:S(2)}, u32[]{:S(2)}) %all-to-all-start) | async-done | bytes 327712 | tf_op jit(solution)/shard_map/all_to_all | solution.py:95
  23.8 0.7 fusion.33
  24.5 3.6 %all-to-all-start.1 = ((bf16[8,48,256]{2,1,0:T(8,128)(2,1)}), bf16[8,48,256]{2,1,0:T(8,128)(2,1)S(1)}, u32[]{:S(2)}, u32[]{:S(2)}) async-start(bf16[8,48,256]{2,1,0:T(8,128)(2,1)} %fusion.33), calls=%async_computation.1 | async-start | bytes 393216 | tf_op jit(solution)/shard_map/all_to_all | solution.py:132
  28.1 7.8 %all-to-all-done.1 = bf16[8,48,256]{2,1,0:T(8,128)(2,1)S(1)} async-done(((bf16[8,48,256]{2,1,0:T(8,128)(2,1)}), bf16[8,48,256]{2,1,0:T(8,128)(2,1)S(1)}, u32[]{:S(2)}, u32[]{:S(2)}) %all-to-all-start.1) | async-done | bytes 196640 | tf_op jit(solution)/shard_map/all_to_all | solution.py:132
  36.0 10.1 %psum.7 = f32[8,384]{1,0:T(8,128)S(1)} all-reduce(f32[8,384]{1,0:T(8,128)S(1)} %pad_maximum_fusion.16), channel_id=1, replica_groups=mesh['group'=4,'dev'=8] {'group'}, use_global_device_ids=true, to_apply=%region_3.4 | all-reduce | flops 3072 | bytes 24576 | tf_op jit(solution)/shard_map/psum | solution.py:143
  48.6 1.7 %multiply_convert_fusion.1 = (bf16[520,512]{1,0:T(8,128)(2,1)S(1)}, bf16[520,512]{1,0:T(8,128)(2,1)}) fusion(bf16[8,512]{1,0:T(8,128)(2,1)S(1)} %copy-done.14, bf16[512,512]{1,0:T(8,128)(2,1)S(1)} %copy-done.11, bf16[8,512]{1,0:T(8,128)(2,1)S(1)} %copy-done.10, bf16[512,512]{1,0:T(8,128)(2,1)S(1)} %copy-done.12, bf16[520,512]{1,0:T(8,128)(2,1)S(1)} %fusion.5, ...), kind=kOutput, calls=%fused_computation.26 | convolution fusion | flops 277954560 | bytes 3186688 | tf_op jit(solution)/shard_map/dot_general | solution.py:16
  51.8 0.7 pad_maximum_fusion.9
  52.5 3.4 %all-to-all-start.2 = ((bf16[8,40,256]{2,1,0:T(8,128)(2,1)}), bf16[8,40,256]{2,1,0:T(8,128)(2,1)S(1)}, u32[]{:S(2)}, u32[]{:S(2)}) async-start(bf16[8,40,256]{2,1,0:T(8,128)(2,1)} %pad_maximum_fusion.9), calls=%async_computation.2 | async-start | bytes 327680 | tf_op jit(solution)/shard_map/all_to_all | solution.py:167
  57.7 1.7 %fusion.12 = f32[512,512]{1,0:T(8,128)} fusion(bf16[520,512]{1,0:T(8,128)(2,1)S(1)} %copy-done.16, bf16[520,512]{1,0:T(8,128)(2,1)S(1)} %copy-done.18, f32[520]{0:T(1024)S(1)} %fusion.44), kind=kOutput, calls=%fused_computation.32 | convolution fusion | flops 273428480 | bytes 2115616 | tf_op jit(solution)/shard_map/dot_general | solution.py:16
  59.3 4.1 %all-to-all-done.2 = bf16[8,40,256]{2,1,0:T(8,128)(2,1)S(1)} async-done(((bf16[8,40,256]{2,1,0:T(8,128)(2,1)}), bf16[8,40,256]{2,1,0:T(8,128)(2,1)S(1)}, u32[]{:S(2)}, u32[]{:S(2)}) %all-to-all-start.2) | async-done | bytes 163872 | tf_op jit(solution)/shard_map/all_to_all | solution.py:167
  64.7 0.8 copy-done.3
  65.9 2.0 %collective-permute-done = bf16[512,512]{1,0:T(8,128)(2,1)} collective-permute-done((bf16[512,512]{1,0:T(8,128)(2,1)S(1)}, bf16[512,512]{1,0:T(8,128)(2,1)}, u32[]{:S(2)}, u32[]{:S(2)}) %collective-permute-start) | collective-permute-done | bytes 524320 | tf_op jit(solution)/shard_map/ppermute | solution.py:51
  67.9 1.2 %bitcast_add_fusion = f32[512,512]{1,0:T(8,128)S(1)} fusion(bf16[512,512]{1,0:T(8,128)(2,1)} %collective-permute-done, f32[2,512,512]{2,1,0:T(8,128)S(1)} %bitcast.66, s32[]{:T(128)S(6)} %select_n.70), kind=kLoop, calls=%fused_computation.30 | loop fusion | flops 524288 | bytes 2621444 | tf_op jit(solution)/shard_map/add | solution.py:51
  69.1 1.0 copy-done.1
  70.1 1.6 %collective-permute-start.1 = (bf16[256,512]{1,0:T(8,128)(2,1)S(1)}, bf16[256,512]{1,0:T(8,128)(2,1)S(1)}, u32[]{:S(2)}, u32[]{:S(2)}) collective-permute-start(bf16[256,512]{1,0:T(8,128)(2,1)S(1)} %fusion.23), channel_id=1, source_target_pairs={{0,16},{8,24},{16,0},{24,8},{1,17},{9,25},{17,1},{25,9},{2,18},{10... | collective-permute-start | bytes 786440 | tf_op jit(solution)/shard_map/ppermute | solution.py:51
  71.7 6.8 %collective-permute-done.1 = bf16[256,512]{1,0:T(8,128)(2,1)S(1)} collective-permute-done((bf16[256,512]{1,0:T(8,128)(2,1)S(1)}, bf16[256,512]{1,0:T(8,128)(2,1)S(1)}, u32[]{:S(2)}, u32[]{:S(2)}) %collective-permute-start.1) | collective-permute-done | bytes 262176 | tf_op jit(solution)/shard_map/ppermute | solution.py:51
  78.6 1.1 fusion.15
  79.7 11.1 %all_to_all.25 = bf16[8,32,512]{2,1,0:T(8,128)(2,1)S(1)} all-to-all(bf16[8,32,512]{2,1,0:T(8,128)(2,1)S(1)} %bitcast.74), channel_id=1, replica_groups=mesh['group'=4,'dev'=8] {'dev'}, dimensions={0} | all-to-all | bytes 524288 | tf_op jit(solution)/shard_map/all_to_all | solution.py:41
  90.8 11.9 %all_to_all.26 = bf16[8,32,512]{2,1,0:T(8,128)(2,1)S(1)} all-to-all(bf16[8,32,512]{2,1,0:T(8,128)(2,1)S(1)} %broadcast_in_dim.32), channel_id=1, replica_groups=mesh['group'=4,'dev'=8] {'dev'}, dimensions={0} | all-to-all | bytes 524288 | tf_op jit(solution)/shard_map/all_to_all | solution.py:41
  102.7 1.5 %collective-permute-start.2 = (bf16[256,512]{1,0:T(8,128)(2,1)S(1)}, bf16[256,512]{1,0:T(8,128)(2,1)S(1)}, u32[]{:S(2)}, u32[]{:S(2)}) collective-permute-start(bf16[256,512]{1,0:T(8,128)(2,1)S(1)} %bitcast.73), channel_id=1, source_target_pairs={{0,16},{8,24},{16,0},{24,8},{1,17},{9,25},{17,1},{25,9},{2,18},{10... | collective-permute-start | bytes 786440 | tf_op jit(solution)/shard_map/ppermute | solution.py:29
  104.3 4.8 %collective-permute-done.2 = bf16[256,512]{1,0:T(8,128)(2,1)S(1)} collective-permute-done((bf16[256,512]{1,0:T(8,128)(2,1)S(1)}, bf16[256,512]{1,0:T(8,128)(2,1)S(1)}, u32[]{:S(2)}, u32[]{:S(2)}) %collective-permute-start.2) | collective-permute-done | bytes 262176 | tf_op jit(solution)/shard_map/ppermute | solution.py:29
  109.3 0.8 slice.131
  111.5 0.8 slice.141
  112.3 1.0 slice_bitcast_fusion
  113.4 0.8 pad_maximum_fusion.3
  (100 shorter events, 10.4 us)
Async XLA Ops:
  0.6 47.3 %copy-start = (bf16[512,512]{1,0:T(8,128)(2,1)S(1)}, bf16[512,512]{1,0:T(8,128)(2,1)}, u32[]{:S(2)}) copy-start(bf16[512,512]{1,0:T(8,128)(2,1)} %param.16) | copy-start | bytes 1572868
  2.3 10.2 %copy-start.8 = (s32[4096]{0:T(1024)S(1)}, s32[4096]{0:T(1024)}, u32[]{:S(2)}) copy-start(s32[4096]{0:T(1024)} %param.18) | copy-start | bytes 49156
  2.3 10.2 %copy-start.9 = (s32[4096]{0:T(1024)S(1)}, s32[4096]{0:T(1024)}, u32[]{:S(2)}) copy-start(s32[4096]{0:T(1024)} %param.19) | copy-start | bytes 49156
  2.3 10.2 %copy-start.13 = (s32[4096]{0:T(1024)S(1)}, s32[4096]{0:T(1024)}, u32[]{:S(2)}) copy-start(s32[4096]{0:T(1024)} %param.17) | copy-start | bytes 49156
  5.2 17.6 %all-to-all-start = ((bf16[8,40,512]{2,1,0:T(8,128)(2,1)}), bf16[8,40,512]{2,1,0:T(8,128)(2,1)S(1)}, u32[]{:S(2)}, u32[]{:S(2)}) async-start(bf16[8,40,512]{2,1,0:T(8,128)(2,1)} %pad_maximum_fusion.4), calls=%async_computation | async-start | bytes 655360 | tf_op jit(solution)/shard_map/all_to_all | solution.py:95
  12.5 10.3 %copy-start.7 = (bf16[512,256]{1,0:T(8,128)(2,1)S(1)}, bf16[512,256]{1,0:T(8,128)(2,1)}, u32[]{:S(2)}) copy-start(bf16[512,256]{1,0:T(8,128)(2,1)} %param.14) | copy-start | bytes 786436
  14.5 8.9 %copy-start.5 = (f32[320,320]{0,1:T(8,128)}, f32[320,320]{0,1:T(8,128)S(1)}, u32[]{:S(2)}) copy-start(f32[320,320]{0,1:T(8,128)S(1)} %get-tuple-element.16) | copy-start | bytes 1228804
  23.8 23.1 %copy-start.2 = (bf16[256,512]{1,0:T(8,128)(2,1)S(1)}, bf16[256,512]{1,0:T(8,128)(2,1)}, u32[]{:S(2)}) copy-start(bf16[256,512]{1,0:T(8,128)(2,1)} %param.15) | copy-start | bytes 786436
  24.5 11.4 %all-to-all-start.1 = ((bf16[8,48,256]{2,1,0:T(8,128)(2,1)}), bf16[8,48,256]{2,1,0:T(8,128)(2,1)S(1)}, u32[]{:S(2)}, u32[]{:S(2)}) async-start(bf16[8,48,256]{2,1,0:T(8,128)(2,1)} %fusion.33), calls=%async_computation.1 | async-start | bytes 393216 | tf_op jit(solution)/shard_map/all_to_all | solution.py:132
  46.5 0.7 copy-start.10
  46.5 1.1 copy-start.12
  47.6 1.0 copy-start.11
  47.6 1.0 copy-start.14
  48.6 1.7 %copy-start.15 = (bf16[520,512]{1,0:T(8,128)(2,1)}, bf16[520,512]{1,0:T(8,128)(2,1)S(1)}, u32[]{:S(2)}) copy-start(bf16[520,512]{1,0:T(8,128)(2,1)S(1)} %fusion.5) | copy-start | bytes 1597444
  50.3 0.8 copy-start.17
  52.5 10.9 %all-to-all-start.2 = ((bf16[8,40,256]{2,1,0:T(8,128)(2,1)}), bf16[8,40,256]{2,1,0:T(8,128)(2,1)S(1)}, u32[]{:S(2)}, u32[]{:S(2)}) async-start(bf16[8,40,256]{2,1,0:T(8,128)(2,1)} %pad_maximum_fusion.9), calls=%async_computation.2 | async-start | bytes 327680 | tf_op jit(solution)/shard_map/all_to_all | solution.py:167
  56.5 1.1 copy-start.16
  56.5 1.2 %copy-start.18 = (bf16[520,512]{1,0:T(8,128)(2,1)S(1)}, bf16[520,512]{1,0:T(8,128)(2,1)}, u32[]{:S(2)}) copy-start(bf16[520,512]{1,0:T(8,128)(2,1)} %copy-done.17) | copy-start | bytes 1597444
  57.7 5.8 %copy-start.6 = (f32[320,320]{0,1:T(8,128)S(1)}, f32[320,320]{0,1:T(8,128)}, u32[]{:S(2)}) copy-start(f32[320,320]{0,1:T(8,128)} %copy-done.5) | copy-start | bytes 1228804
  64.3 1.2 %copy-start.3 = (f32[512,512]{1,0:T(8,128)S(1)}, f32[512,512]{1,0:T(8,128)}, u32[]{:S(2)}) copy-start(f32[512,512]{1,0:T(8,128)} %fusion.12) | copy-start | bytes 3145732
  65.8 2.1 %collective-permute-start = (bf16[512,512]{1,0:T(8,128)(2,1)S(1)}, bf16[512,512]{1,0:T(8,128)(2,1)}, u32[]{:S(2)}, u32[]{:S(2)}) collective-permute-start(bf16[512,512]{1,0:T(8,128)(2,1)S(1)} %fusion.14), channel_id=1, source_target_pairs={{0,8},{8,0},{16,24},{24,16},{1,9},{9,1},{17,25},{25,17},{2,10},{10... | collective-permute-start | bytes 1572872 | tf_op jit(solution)/shard_map/ppermute | solution.py:51
  69.1 1.0 copy-start.1
  70.1 8.4 %collective-permute-start.1 = (bf16[256,512]{1,0:T(8,128)(2,1)S(1)}, bf16[256,512]{1,0:T(8,128)(2,1)S(1)}, u32[]{:S(2)}, u32[]{:S(2)}) collective-permute-start(bf16[256,512]{1,0:T(8,128)(2,1)S(1)} %fusion.23), channel_id=1, source_target_pairs={{0,16},{8,24},{16,0},{24,8},{1,17},{9,25},{17,1},{25,9},{2,18},{10... | collective-permute-start | bytes 786440 | tf_op jit(solution)/shard_map/ppermute | solution.py:51
  102.7 6.6 %copy-start.4 = (bf16[520,512]{1,0:T(8,128)(2,1)S(1)}, bf16[520,512]{1,0:T(8,128)(2,1)}, u32[]{:S(2)}) copy-start(bf16[520,512]{1,0:T(8,128)(2,1)} %get-tuple-element.8) | copy-start | bytes 1597444
  102.7 6.4 %collective-permute-start.2 = (bf16[256,512]{1,0:T(8,128)(2,1)S(1)}, bf16[256,512]{1,0:T(8,128)(2,1)S(1)}, u32[]{:S(2)}, u32[]{:S(2)}) collective-permute-start(bf16[256,512]{1,0:T(8,128)(2,1)S(1)} %bitcast.73), channel_id=1, source_target_pairs={{0,16},{8,24},{16,0},{24,8},{1,17},{9,25},{17,1},{25,9},{2,18},{10... | collective-permute-start | bytes 786440 | tf_op jit(solution)/shard_map/ppermute | solution.py:29
  109.2 2.0 %collective-permute-start.3 = (bf16[512,512]{1,0:T(8,128)(2,1)S(1)}, bf16[512,512]{1,0:T(8,128)(2,1)S(1)}, u32[]{:S(2)}, u32[]{:S(2)}) collective-permute-start(bf16[512,512]{1,0:T(8,128)(2,1)S(1)} %bitcast.72), channel_id=1, source_target_pairs={{0,8},{8,0},{16,24},{24,16},{1,9},{9,1},{17,25},{25,17},{2,10},{10... | collective-permute-start | bytes 1572872 | tf_op jit(solution)/shard_map/ppermute | solution.py:29
where the time goes:
time: 115 us; the launch traced here: 114 us
  waiting for transfers between devices  33.9 us (29%)
  blocking collectives  33.1 us (29%)
  starting transfers between devices  17.5 us (15%)
  matrix products  12.1 us (11%)
  local copies, waits for them, and re-layouts  9.5 us (8%)
  other arithmetic  6.87 us (6%)
    all_to_all x2, blocking collectives, swap(): lax.all_to_all(blocks, axis, 0, 0, tiled=True, axis_index_groups=groups)  23 us
    dot_general x20, matrix products, dot(): lax.dot_general(left, right, (dims, ((), ())), preferred_element_type=F32)  12.1 us
    psum x1, blocking collectives, shards(): hub_sums = lax.psum(hub_sums, 'group')  10.1 us
    ppermute x2, waiting for transfers between devices, scatter_sum(): return own + lax.ppermute(sent, axis, pairs).astype(F32)  8.81 us
    all_to_all x1, waiting for transfers between devices, shards(): arrived = lax.all_to_all(packed, 'dev', 0, 0, tiled=True)  7.98 us
    all_to_all x1, waiting for transfers between devices, shards(): back = lax.all_to_all(message, 'dev', 0, 0, tiled=True)  7.78 us
    all_to_all x1, starting transfers between devices, shards(): arrived = lax.all_to_all(packed, 'dev', 0, 0, tiled=True)  7.25 us
    ppermute x2, waiting for transfers between devices, swap(): lax.ppermute(lax.dynamic_index_in_dim(blocks, 1 - position, 0, False), ax...  5.28 us
  transfers between devices with their start and end apart: 7, of which 7 were waited for; matrix products, arithmetic and copies ran while one was open for 6% of the time, Pallas kernels for 0%

commit v1 on v0

--- a/solution.py
+++ b/solution.py
@@ -140,7 +140,7 @@
     hub_sums = jnp.concatenate(
         [hub_hidden, jnp.broadcast_to(hub_degree[:, None], (hub_rows, 128))], axis=1
     )
-    hub_sums = lax.psum(hub_sums, "group")
+    hub_sums = jnp.sum(lax.all_gather(hub_sums, "group"), axis=0)
     hub_hidden, hub_degree = (
         hub_sums[:, :hidden_width],
         hub_sums[:, hidden_width : hidden_width + 1],

time: 115 us -> 111 us (0.965)
  blocking collectives: 33.1 us -> 28.2 us
    psum x1 -> x0, blocking collectives: 10.1 us -> none  [shards(): hub_sums = lax.psum(hub_sums, 'group')]
    all_gather x0 -> x1, blocking collectives: none -> 5.21 us  [shards(): hub_sums = jnp.sum(lax.all_gather(hub_sums, 'group'), axis=0)]
where the time goes in v1:
time: 111 us; the launch traced here: 110 us
  waiting for transfers between devices  34.7 us (31%)
  blocking collectives  28.2 us (25%)
  starting transfers between devices  17.5 us (16%)
  matrix products  12.1 us (11%)
  local copies, waits for them, and re-layouts  9.51 us (9%)
  other arithmetic  6.88 us (6%)
  between operations  1.15 us (1%)
    all_to_all x2, blocking collectives, swap(): lax.all_to_all(blocks, axis, 0, 0, tiled=True, axis_index_groups=groups)  23 us
    dot_general x20, matrix products, dot(): lax.dot_general(left, right, (dims, ((), ())), preferred_element_type=F32)  12.1 us
    ppermute x2, waiting for transfers between devices, scatter_sum(): return own + lax.ppermute(sent, axis, pairs).astype(F32)  8.84 us
    all_to_all x1, waiting for transfers between devices, shards(): arrived = lax.all_to_all(packed, 'dev', 0, 0, tiled=True)  7.98 us
    all_to_all x1, waiting for transfers between devices, shards(): back = lax.all_to_all(message, 'dev', 0, 0, tiled=True)  7.78 us
    all_to_all x1, starting transfers between devices, shards(): arrived = lax.all_to_all(packed, 'dev', 0, 0, tiled=True)  7.25 us
    ppermute x2, waiting for transfers between devices, swap(): lax.ppermute(lax.dynamic_index_in_dim(blocks, 1 - position, 0, False), ax...  5.31 us
    all_gather x1, blocking collectives, shards(): hub_sums = jnp.sum(lax.all_gather(hub_sums, 'group'), axis=0)  5.21 us
  transfers between devices with their start and end apart: 7, of which 7 were waited for; matrix products, arithmetic and copies ran while one was open for 6% of the time, Pallas kernels for 0%

profile of v1, /device:TPU:0, one launch (start us, length us, event | category | flops | bytes accessed | tf_op | source)
XLA Modules:
  0.0 110.0 jit_solution(7161202210810332820)
XLA Ops:
  0.6 0.8 iota_compare_fusion.11
  1.5 0.8 squeeze.19
  2.3 1.4 %convolution_convert_fusion.1 = bf16[256,512]{1,0:T(8,128)(2,1)S(1)} fusion(bf16[512,512]{1,0:T(8,128)(2,1)} %param.12, s32[256]{0:T(256)S(1)} %broadcast_select_fusion), kind=kOutput, calls=%fused_computation.16 | convolution fusion | flops 134479872 | bytes 787456 | tf_op jit(solution)/shard_map/dot_general | solution.py:16
  3.7 0.7 broadcast_in_dim.28
  4.4 0.7 pad_maximum_fusion.4
  5.2 7.3 %all-to-all-start = ((bf16[8,40,512]{2,1,0:T(8,128)(2,1)}), bf16[8,40,512]{2,1,0:T(8,128)(2,1)S(1)}, u32[]{:S(2)}, u32[]{:S(2)}) async-start(bf16[8,40,512]{2,1,0:T(8,128)(2,1)} %pad_maximum_fusion.4), calls=%async_computation | async-start | bytes 655360 | tf_op jit(solution)/shard_map/all_to_all | solution.py:95
  12.5 2.0 %fusion.62 = (f32[320]{0:T(512)S(1)}, f32[320,320]{0,1:T(8,128)S(1)}) fusion(s32[4096]{0:T(1024)S(1)} %copy-done.13, s32[4096]{0:T(1024)S(1)} %compare_select_fusion), kind=kOutput, calls=%fused_computation.121 | convolution fusion | flops 841584320 | bytes 443648 | tf_op jit(solution)/shard_map/dot_general | solution.py:16
  14.8 8.0 %all-to-all-done = bf16[8,40,512]{2,1,0:T(8,128)(2,1)S(1)} async-done(((bf16[8,40,512]{2,1,0:T(8,128)(2,1)}), bf16[8,40,512]{2,1,0:T(8,128)(2,1)S(1)}, u32[]{:S(2)}, u32[]{:S(2)}) %all-to-all-start) | async-done | bytes 327712 | tf_op jit(solution)/shard_map/all_to_all | solution.py:95
  23.8 0.7 fusion.33
  24.5 3.6 %all-to-all-start.1 = ((bf16[8,48,256]{2,1,0:T(8,128)(2,1)}), bf16[8,48,256]{2,1,0:T(8,128)(2,1)S(1)}, u32[]{:S(2)}, u32[]{:S(2)}) async-start(bf16[8,48,256]{2,1,0:T(8,128)(2,1)} %fusion.33), calls=%async_computation.1 | async-start | bytes 393216 | tf_op jit(solution)/shard_map/all_to_all | solution.py:132
  28.1 7.8 %all-to-all-done.1 = bf16[8,48,256]{2,1,0:T(8,128)(2,1)S(1)} async-done(((bf16[8,48,256]{2,1,0:T(8,128)(2,1)}), bf16[8,48,256]{2,1,0:T(8,128)(2,1)S(1)}, u32[]{:S(2)}, u32[]{:S(2)}) %all-to-all-start.1) | async-done | bytes 196640 | tf_op jit(solution)/shard_map/all_to_all | solution.py:132
  36.0 5.2 %all-gather = f32[32,384]{1,0:T(8,128)S(1)} all-gather(f32[8,384]{1,0:T(8,128)S(1)} %pad_maximum_fusion.16), channel_id=2, replica_groups=mesh['group'=4,'dev'=8] {'group'}, dimensions={0}, use_global_device_ids=true | all-gather | bytes 61440 | tf_op jit(solution)/shard_map/all_gather | solution.py:143
  43.7 1.7 %multiply_convert_fusion.1 = (bf16[520,512]{1,0:T(8,128)(2,1)S(1)}, bf16[520,512]{1,0:T(8,128)(2,1)}) fusion(bf16[8,512]{1,0:T(8,128)(2,1)S(1)} %copy-done.14, bf16[512,512]{1,0:T(8,128)(2,1)S(1)} %copy-done.11, bf16[8,512]{1,0:T(8,128)(2,1)S(1)} %copy-done.10, bf16[512,512]{1,0:T(8,128)(2,1)S(1)} %copy-done.12, bf16[520,512]{1,0:T(8,128)(2,1)S(1)} %fusion.5, ...), kind=kOutput, calls=%fused_computation.26 | convolution fusion | flops 277954560 | bytes 3186688 | tf_op jit(solution)/shard_map/dot_general | solution.py:16
  46.9 0.7 pad_maximum_fusion.9
  47.6 3.4 %all-to-all-start.2 = ((bf16[8,40,256]{2,1,0:T(8,128)(2,1)}), bf16[8,40,256]{2,1,0:T(8,128)(2,1)S(1)}, u32[]{:S(2)}, u32[]{:S(2)}) async-start(bf16[8,40,256]{2,1,0:T(8,128)(2,1)} %pad_maximum_fusion.9), calls=%async_computation.2 | async-start | bytes 327680 | tf_op jit(solution)/shard_map/all_to_all | solution.py:167
  52.8 1.7 %fusion.12 = f32[512,512]{1,0:T(8,128)} fusion(bf16[520,512]{1,0:T(8,128)(2,1)S(1)} %copy-done.16, bf16[520,512]{1,0:T(8,128)(2,1)S(1)} %copy-done.18, f32[520]{0:T(1024)S(1)} %fusion.44), kind=kOutput, calls=%fused_computation.32 | convolution fusion | flops 273428480 | bytes 2115616 | tf_op jit(solution)/shard_map/dot_general | solution.py:16
  54.4 4.8 %all-to-all-done.2 = bf16[8,40,256]{2,1,0:T(8,128)(2,1)S(1)} async-done(((bf16[8,40,256]{2,1,0:T(8,128)(2,1)}), bf16[8,40,256]{2,1,0:T(8,128)(2,1)S(1)}, u32[]{:S(2)}, u32[]{:S(2)}) %all-to-all-start.2) | async-done | bytes 163872 | tf_op jit(solution)/shard_map/all_to_all | solution.py:167
  60.5 0.8 copy-done.3
  61.7 2.0 %collective-permute-done = bf16[512,512]{1,0:T(8,128)(2,1)} collective-permute-done((bf16[512,512]{1,0:T(8,128)(2,1)S(1)}, bf16[512,512]{1,0:T(8,128)(2,1)}, u32[]{:S(2)}, u32[]{:S(2)}) %collective-permute-start) | collective-permute-done | bytes 524320 | tf_op jit(solution)/shard_map/ppermute | solution.py:51
  63.7 1.2 %bitcast_add_fusion = f32[512,512]{1,0:T(8,128)S(1)} fusion(bf16[512,512]{1,0:T(8,128)(2,1)} %collective-permute-done, f32[2,512,512]{2,1,0:T(8,128)S(1)} %bitcast.68, s32[]{:T(128)S(6)} %select_n.70), kind=kLoop, calls=%fused_computation.30 | loop fusion | flops 524288 | bytes 2621444 | tf_op jit(solution)/shard_map/add | solution.py:51
  64.9 1.0 copy-done.1
  65.9 1.6 %collective-permute-start.1 = (bf16[256,512]{1,0:T(8,128)(2,1)S(1)}, bf16[256,512]{1,0:T(8,128)(2,1)S(1)}, u32[]{:S(2)}, u32[]{:S(2)}) collective-permute-start(bf16[256,512]{1,0:T(8,128)(2,1)S(1)} %fusion.23), channel_id=1, source_target_pairs={{0,16},{8,24},{16,0},{24,8},{1,17},{9,25},{17,1},{25,9},{2,18},{10... | collective-permute-start | bytes 786440 | tf_op jit(solution)/shard_map/ppermute | solution.py:51
  67.5 6.8 %collective-permute-done.1 = bf16[256,512]{1,0:T(8,128)(2,1)S(1)} collective-permute-done((bf16[256,512]{1,0:T(8,128)(2,1)S(1)}, bf16[256,512]{1,0:T(8,128)(2,1)S(1)}, u32[]{:S(2)}, u32[]{:S(2)}) %collective-permute-start.1) | collective-permute-done | bytes 262176 | tf_op jit(solution)/shard_map/ppermute | solution.py:51
  74.3 1.1 %fusion.15 = bf16[256,512]{1,0:T(8,128)(2,1)S(1)} fusion(bf16[256,512]{1,0:T(8,128)(2,1)S(1)} %collective-permute-done.1, f32[2,256,512]{2,1,0:T(8,128)} %bitcast.73, s32[]{:T(128)S(6)} %select_n.72), kind=kLoop, calls=%fused_computation.42 | loop fusion | flops 393216 | bytes 1048580 | tf_op jit(solution)/shard_map/convert_element_type | solution.py:52
  75.4 11.2 %all_to_all.25 = bf16[8,32,512]{2,1,0:T(8,128)(2,1)S(1)} all-to-all(bf16[8,32,512]{2,1,0:T(8,128)(2,1)S(1)} %bitcast.76), channel_id=1, replica_groups=mesh['group'=4,'dev'=8] {'dev'}, dimensions={0} | all-to-all | bytes 524288 | tf_op jit(solution)/shard_map/all_to_all | solution.py:41
  86.7 11.8 %all_to_all.26 = bf16[8,32,512]{2,1,0:T(8,128)(2,1)S(1)} all-to-all(bf16[8,32,512]{2,1,0:T(8,128)(2,1)S(1)} %broadcast_in_dim.32), channel_id=1, replica_groups=mesh['group'=4,'dev'=8] {'dev'}, dimensions={0} | all-to-all | bytes 524288 | tf_op jit(solution)/shard_map/all_to_all | solution.py:41
  98.5 1.5 %collective-permute-start.2 = (bf16[256,512]{1,0:T(8,128)(2,1)S(1)}, bf16[256,512]{1,0:T(8,128)(2,1)S(1)}, u32[]{:S(2)}, u32[]{:S(2)}) collective-permute-start(bf16[256,512]{1,0:T(8,128)(2,1)S(1)} %bitcast.75), channel_id=1, source_target_pairs={{0,16},{8,24},{16,0},{24,8},{1,17},{9,25},{17,1},{25,9},{2,18},{10... | collective-permute-start | bytes 786440 | tf_op jit(solution)/shard_map/ppermute | solution.py:29
  100.0 4.9 %collective-permute-done.2 = bf16[256,512]{1,0:T(8,128)(2,1)S(1)} collective-permute-done((bf16[256,512]{1,0:T(8,128)(2,1)S(1)}, bf16[256,512]{1,0:T(8,128)(2,1)S(1)}, u32[]{:S(2)}, u32[]{:S(2)}) %collective-permute-start.2) | collective-permute-done | bytes 262176 | tf_op jit(solution)/shard_map/ppermute | solution.py:29
  105.1 0.8 slice.131
  107.3 0.8 slice.141
  108.1 1.0 slice_bitcast_fusion
  109.2 0.8 pad_maximum_fusion.3
  (101 shorter events, 10.4 us)
Async XLA Ops:
  0.6 42.4 %copy-start = (bf16[512,512]{1,0:T(8,128)(2,1)S(1)}, bf16[512,512]{1,0:T(8,128)(2,1)}, u32[]{:S(2)}) copy-start(bf16[512,512]{1,0:T(8,128)(2,1)} %param.16) | copy-start | bytes 1572868
  2.3 10.2 %copy-start.8 = (s32[4096]{0:T(1024)S(1)}, s32[4096]{0:T(1024)}, u32[]{:S(2)}) copy-start(s32[4096]{0:T(1024)} %param.18) | copy-start | bytes 49156
  2.3 10.2 %copy-start.9 = (s32[4096]{0:T(1024)S(1)}, s32[4096]{0:T(1024)}, u32[]{:S(2)}) copy-start(s32[4096]{0:T(1024)} %param.19) | copy-start | bytes 49156
  2.3 10.2 %copy-start.13 = (s32[4096]{0:T(1024)S(1)}, s32[4096]{0:T(1024)}, u32[]{:S(2)}) copy-start(s32[4096]{0:T(1024)} %param.17) | copy-start | bytes 49156
  5.2 17.6 %all-to-all-start = ((bf16[8,40,512]{2,1,0:T(8,128)(2,1)}), bf16[8,40,512]{2,1,0:T(8,128)(2,1)S(1)}, u32[]{:S(2)}, u32[]{:S(2)}) async-start(bf16[8,40,512]{2,1,0:T(8,128)(2,1)} %pad_maximum_fusion.4), calls=%async_computation | async-start | bytes 655360 | tf_op jit(solution)/shard_map/all_to_all | solution.py:95
  12.5 10.3 %copy-start.7 = (bf16[512,256]{1,0:T(8,128)(2,1)S(1)}, bf16[512,256]{1,0:T(8,128)(2,1)}, u32[]{:S(2)}) copy-start(bf16[512,256]{1,0:T(8,128)(2,1)} %param.14) | copy-start | bytes 786436
  14.5 8.9 %copy-start.5 = (f32[320,320]{0,1:T(8,128)}, f32[320,320]{0,1:T(8,128)S(1)}, u32[]{:S(2)}) copy-start(f32[320,320]{0,1:T(8,128)S(1)} %get-tuple-element.16) | copy-start | bytes 1228804
  23.8 18.2 %copy-start.2 = (bf16[256,512]{1,0:T(8,128)(2,1)S(1)}, bf16[256,512]{1,0:T(8,128)(2,1)}, u32[]{:S(2)}) copy-start(bf16[256,512]{1,0:T(8,128)(2,1)} %param.15) | copy-start | bytes 786436
  24.5 11.4 %all-to-all-start.1 = ((bf16[8,48,256]{2,1,0:T(8,128)(2,1)}), bf16[8,48,256]{2,1,0:T(8,128)(2,1)S(1)}, u32[]{:S(2)}, u32[]{:S(2)}) async-start(bf16[8,48,256]{2,1,0:T(8,128)(2,1)} %fusion.33), calls=%async_computation.1 | async-start | bytes 393216 | tf_op jit(solution)/shard_map/all_to_all | solution.py:132
  41.6 0.7 copy-start.10
  41.6 1.1 copy-start.12
  42.7 1.0 copy-start.11
  42.7 1.0 copy-start.14
  43.7 1.7 %copy-start.15 = (bf16[520,512]{1,0:T(8,128)(2,1)}, bf16[520,512]{1,0:T(8,128)(2,1)S(1)}, u32[]{:S(2)}) copy-start(bf16[520,512]{1,0:T(8,128)(2,1)S(1)} %fusion.5) | copy-start | bytes 1597444
  45.4 0.8 copy-start.17
  47.6 11.6 %all-to-all-start.2 = ((bf16[8,40,256]{2,1,0:T(8,128)(2,1)}), bf16[8,40,256]{2,1,0:T(8,128)(2,1)S(1)}, u32[]{:S(2)}, u32[]{:S(2)}) async-start(bf16[8,40,256]{2,1,0:T(8,128)(2,1)} %pad_maximum_fusion.9), calls=%async_computation.2 | async-start | bytes 327680 | tf_op jit(solution)/shard_map/all_to_all | solution.py:167
  51.6 1.0 copy-start.16
  51.6 1.2 %copy-start.18 = (bf16[520,512]{1,0:T(8,128)(2,1)S(1)}, bf16[520,512]{1,0:T(8,128)(2,1)}, u32[]{:S(2)}) copy-start(bf16[520,512]{1,0:T(8,128)(2,1)} %copy-done.17) | copy-start | bytes 1597444
  52.8 6.4 %copy-start.6 = (f32[320,320]{0,1:T(8,128)S(1)}, f32[320,320]{0,1:T(8,128)}, u32[]{:S(2)}) copy-start(f32[320,320]{0,1:T(8,128)} %copy-done.5) | copy-start | bytes 1228804
  60.1 1.2 %copy-start.3 = (f32[512,512]{1,0:T(8,128)S(1)}, f32[512,512]{1,0:T(8,128)}, u32[]{:S(2)}) copy-start(f32[512,512]{1,0:T(8,128)} %fusion.12) | copy-start | bytes 3145732
  61.6 2.1 %collective-permute-start = (bf16[512,512]{1,0:T(8,128)(2,1)S(1)}, bf16[512,512]{1,0:T(8,128)(2,1)}, u32[]{:S(2)}, u32[]{:S(2)}) collective-permute-start(bf16[512,512]{1,0:T(8,128)(2,1)S(1)} %fusion.14), channel_id=1, source_target_pairs={{0,8},{8,0},{16,24},{24,16},{1,9},{9,1},{17,25},{25,17},{2,10},{10... | collective-permute-start | bytes 1572872 | tf_op jit(solution)/shard_map/ppermute | solution.py:51
  64.9 1.0 copy-start.1
  65.9 8.4 %collective-permute-start.1 = (bf16[256,512]{1,0:T(8,128)(2,1)S(1)}, bf16[256,512]{1,0:T(8,128)(2,1)S(1)}, u32[]{:S(2)}, u32[]{:S(2)}) collective-permute-start(bf16[256,512]{1,0:T(8,128)(2,1)S(1)} %fusion.23), channel_id=1, source_target_pairs={{0,16},{8,24},{16,0},{24,8},{1,17},{9,25},{17,1},{25,9},{2,18},{10... | collective-permute-start | bytes 786440 | tf_op jit(solution)/shard_map/ppermute | solution.py:51
  98.5 6.6 %copy-start.4 = (bf16[520,512]{1,0:T(8,128)(2,1)S(1)}, bf16[520,512]{1,0:T(8,128)(2,1)}, u32[]{:S(2)}) copy-start(bf16[520,512]{1,0:T(8,128)(2,1)} %get-tuple-element.8) | copy-start | bytes 1597444
  98.5 6.4 %collective-permute-start.2 = (bf16[256,512]{1,0:T(8,128)(2,1)S(1)}, bf16[256,512]{1,0:T(8,128)(2,1)S(1)}, u32[]{:S(2)}, u32[]{:S(2)}) collective-permute-start(bf16[256,512]{1,0:T(8,128)(2,1)S(1)} %bitcast.75), channel_id=1, source_target_pairs={{0,16},{8,24},{16,0},{24,8},{1,17},{9,25},{17,1},{25,9},{2,18},{10... | collective-permute-start | bytes 786440 | tf_op jit(solution)/shard_map/ppermute | solution.py:29
  105.0 2.0 %collective-permute-start.3 = (bf16[512,512]{1,0:T(8,128)(2,1)S(1)}, bf16[512,512]{1,0:T(8,128)(2,1)S(1)}, u32[]{:S(2)}, u32[]{:S(2)}) collective-permute-start(bf16[512,512]{1,0:T(8,128)(2,1)S(1)} %bitcast.74), channel_id=1, source_target_pairs={{0,8},{8,0},{16,24},{24,16},{1,9},{9,1},{17,25},{25,17},{2,10},{10... | collective-permute-start | bytes 1572872 | tf_op jit(solution)/shard_map/ppermute | solution.py:29
